TPU v7x, 256 devices: a whole 4x4x8 slice. The times are simulated.
256 devices in a mesh: tensor: 8 (over x, core), dp: 2 (over y_hi), replica: 16 (over z, y_lo).
Axes of the slice: x: 4, y: 4 (y_hi: 2, y_lo: 2; y = y_hi * 2 + y_lo), z: 8, core: 2. Of those that a mesh axis runs over, the one named last changes fastest.
Arguments:
- hidden_states: bfloat16 [16, 2, 512, 4096], P('replica', 'dp', 'tensor'), may hold values from -18 to 18, as said below
- grad_output: bfloat16 [16, 2, 512, 4096], P('replica', 'dp', 'tensor'), may hold values from -6 to 6
- w_in: bfloat16 [16, 4096, 6144], P('replica', None, 'tensor'), may hold values from -6 to 6
- w_out: bfloat16 [16, 4096, 4096], P('replica', 'tensor'), may hold values from -6 to 6
Outputs:
- input_grad: bfloat16 [16, 2, 512, 4096], P('replica', 'dp', 'tensor')
- synced_in: bfloat16 [4096, 6144], P(('dp', 'replica'), 'tensor')
- synced_out: bfloat16 [4096, 4096], P('tensor', ('dp', 'replica'))
Inputs may be any that keep to these rules, and one draw needn't show every extreme that they name: `hidden_states`: each row holds one token's features.
All inputs are finite; a program needn't handle non-finite values.
Results may differ from a plain program's by a relative error of at most 0.028.
Values may be sent and summed in bfloat16 or wider, within the bound.
A program may use at most 128 MiB of HBM per device.

v0:
```python
import jax
import jax.numpy as jnp
from jax import lax
from jax.sharding import PartitionSpec as P

HQ = 32
HD = 128


LEARN_RATE = 0.5
ROPE_BASE = 500000.0
MASK_VALUE = -1e30


def rope_tables(length, width):
    half_width = width // 2
    frequency = ROPE_BASE ** (-(jnp.arange(half_width, dtype=jnp.float32) * 2.0) / width)
    angles = jnp.arange(length, dtype=jnp.float32)[:, None] * frequency[None, :]
    cosine_table = jnp.concatenate([jnp.cos(angles), jnp.cos(angles)], axis=1)
    sine_table = jnp.concatenate([jnp.sin(angles), jnp.sin(angles)], axis=1)
    return (cosine_table[:, None, :], sine_table[:, None, :])


def rotate(values, cosine_table, sine_table):
    half_width = values.shape[-1] // 2
    lower_half = values[..., :half_width]
    upper_half = values[..., half_width:]
    return values * cosine_table + jnp.concatenate([-upper_half, lower_half], -1) * sine_table


def unrotate(gradient, cosine_table, sine_table):
    half_width = gradient.shape[-1] // 2
    scaled = gradient * sine_table
    return gradient * cosine_table + jnp.concatenate(
        [scaled[..., half_width:], -scaled[..., :half_width]], -1
    )


def contract_rows(left, right):
    return lax.dot_general(
        left, right, (((0,), (0,)), ((), ())), preferred_element_type=jnp.float32
    )


def local(hidden_states, grad_output, w_in, w_out):
    weight_in = w_in[0]
    weight_out = w_out[0]
    width = weight_in.shape[0]
    out_width = weight_out.shape[0]
    heads_q = out_width // HD
    heads_kv = (weight_in.shape[1] - out_width) // (2 * HD)
    group_size = heads_q // heads_kv
    scale_in = width ** (-0.5)
    scale_out = (HQ * HD) ** (-0.5)
    full_inputs, full_upstream = (
        lax.all_gather(hidden_states[0, 0], "tensor", axis=0, tiled=True),
        lax.all_gather(grad_output[0, 0], "tensor", axis=0, tiled=True),
    )
    length = full_inputs.shape[0]
    projected = jnp.dot(full_inputs, weight_in, preferred_element_type=jnp.float32) * scale_in
    cosine_table, sine_table = rope_tables(length, HD)
    query_heads = rotate(
        projected[:, :out_width].reshape(length, heads_q, HD), cosine_table, sine_table
    ).astype(jnp.bfloat16)
    key_heads = rotate(
        projected[:, out_width : out_width + heads_kv * HD].reshape(length, heads_kv, HD),
        cosine_table,
        sine_table,
    ).astype(jnp.bfloat16)
    value_heads = (
        projected[:, out_width + heads_kv * HD :].reshape(length, heads_kv, HD).astype(jnp.bfloat16)
    )
    query_groups = query_heads.reshape(length, heads_kv, group_size, HD)
    scores = jnp.einsum(
        "skgd,tkd->kgst", query_groups, key_heads, preferred_element_type=jnp.float32
    ) * HD ** (-0.5)
    causal = jnp.arange(length)[:, None] >= jnp.arange(length)[None, :]
    scores = jnp.where(causal, scores, MASK_VALUE)
    probabilities = jax.nn.softmax(scores, axis=-1)
    weights = probabilities.astype(jnp.bfloat16)
    context = jnp.einsum(
        "kgst,tkd->skgd", weights, value_heads, preferred_element_type=jnp.float32
    ).astype(jnp.bfloat16)
    dcontext = lax.dot_general(
        full_upstream, weight_out, (((1,), (1,)), ((), ())), preferred_element_type=jnp.float32
    )
    dcontext = (dcontext * scale_out).astype(jnp.bfloat16)
    dcontext_groups = dcontext.reshape(length, heads_kv, group_size, HD)
    dprobs = jnp.einsum(
        "skgd,tkd->kgst", dcontext_groups, value_heads, preferred_element_type=jnp.float32
    )
    dvalue = jnp.einsum(
        "kgst,skgd->tkd", weights, dcontext_groups, preferred_element_type=jnp.float32
    )
    row_delta = jnp.einsum(
        "skgd,skgd->kgs", dcontext_groups, context, preferred_element_type=jnp.float32
    )[..., None]
    dscores = (probabilities * (dprobs - row_delta) * HD ** (-0.5)).astype(jnp.bfloat16)
    dquery = jnp.einsum(
        "kgst,tkd->skgd", dscores, key_heads, preferred_element_type=jnp.float32
    ).reshape(length, heads_q, HD)
    key_grad = jnp.einsum(
        "kgst,skgd->tkd", dscores, query_groups, preferred_element_type=jnp.float32
    )
    dquery = unrotate(dquery, cosine_table, sine_table)
    key_grad = unrotate(key_grad, cosine_table, sine_table)
    dprojected = jnp.concatenate(
        [dquery.reshape(length, -1), key_grad.reshape(length, -1), dvalue.reshape(length, -1)], 1
    ).astype(jnp.bfloat16)
    context_flat = context.reshape(length, out_width)
    input_sum = lax.psum_scatter(
        (
            lax.dot_general(
                dprojected, weight_in, (((1,), (1,)), ((), ())), preferred_element_type=jnp.float32
            )
            * scale_in
        ).astype(jnp.bfloat16),
        "tensor",
        scatter_dimension=0,
        tiled=True,
    )
    input_grad = input_sum[None, None]
    node_count = lax.axis_size("dp")
    replica_count = lax.axis_size("replica")
    grad_in = contract_rows(full_inputs, dprojected) * scale_in
    grad_out = contract_rows(full_upstream, context_flat) * scale_out
    rows_in = weight_in.astype(jnp.float32)
    rows_out = weight_out.astype(jnp.float32).T
    stepped = jnp.concatenate([rows_in, rows_out], 1) / node_count - LEARN_RATE * jnp.concatenate(
        [grad_in, grad_out], 1
    )
    summed = lax.psum_scatter(
        stepped / replica_count, ("dp", "replica"), scatter_dimension=0, tiled=True
    )
    in_columns = weight_in.shape[1]
    synced_in = summed[:, :in_columns].astype(jnp.bfloat16)
    synced_out = summed[:, in_columns:].T.astype(jnp.bfloat16)
    return (input_grad, synced_in, synced_out)


def solution(mesh):
    in_specs = (
        P("replica", "dp", "tensor", None),
        P("replica", "dp", "tensor", None),
        P("replica", None, "tensor"),
        P("replica", "tensor", None),
    )
    out_specs = (
        P("replica", "dp", "tensor", None),
        P(("dp", "replica"), "tensor"),
        P("tensor", ("dp", "replica")),
    )
    return jax.shard_map(local, mesh=mesh, in_specs=in_specs, out_specs=out_specs, check_vma=False)
```

profile of v0, /device:TPU:2, one launch (start us, length us, event | category | flops | bytes accessed | tf_op | source)
XLA Modules:
  0.0 625.4 jit_solution(4963517494850911710)
XLA Ops:
  7.2 0.0 all-gather.5.cloned.1.call-start
  7.2 0.7 all-gather.5.cloned.1.call-update
  7.9 0.0 all-gather.7.cloned.1.call-start
  7.9 0.7 all-gather.7.cloned.1.call-update
  8.6 0.0 reduce-scatter.5.cloned.1.call-start
  8.7 8.7 %copy.7 = bf16[1,4096,768]{1,2,0:T(8,128)(2,1)} copy(bf16[1,4096,768]{2,1,0:T(8,128)(2,1)} %param.6) | data formatting | bytes 12582912 | tf_op args[2]
  17.4 0.8 iota_compare_fusion
  18.2 1.0 fusion.67
  19.2 0.0 copy-start.12
  19.2 27.3 %all-gather.5.cloned.1.call-done = bf16[1,1,512,4096]{3,2,1,0:T(8,128)(2,1)} async-done(((bf16[1,1,64,4096]{3,2,1,0:T(8,128)(2,1)}), bf16[1,1,512,4096]{3,2,1,0:T(8,128)(2,1)}) %all-gather.5.cloned.1.call-update) | async-done | bytes 4194320 | tf_op jit(solution)/shard_map/all_gather | solution.py:56
  46.5 7.2 %fusion.26 = f32[512,768]{1,0:T(8,128)S(1)} fusion(bf16[1,4096,768]{2,1,0:T(8,128)(2,1)} %param.6, bf16[1,1,512,4096]{3,2,1,0:T(8,128)(2,1)} %all-gather.5.cloned.1.call-done), kind=kOutput, calls=%fused_computation.33 | convolution fusion | flops 3221618688 | bytes 12058624 | tf_op jit(solution)/shard_map/dot_general | solution.py:60
  53.7 0.0 copy-start.2
  53.7 0.1 fusion.62
  53.9 0.0 copy-done.12
  53.9 1.0 copy-done.2
  54.9 0.3 pad_maximum_fusion.4
  55.1 0.0 slice-start.2
  55.1 0.1 copy.8
  55.3 0.0 copy-start.10
  55.3 0.8 copy.12
  56.1 0.1 mul.167
  56.3 0.3 copy.44
  56.6 0.3 copy.52
  56.9 0.1 slice_negate_fusion.1
  57.1 1.1 maximum_multiply_fusion.1
  58.1 1.3 copy.45
  59.5 2.8 fusion.16
  62.3 2.0 copy-done
  64.3 0.9 fusion.15
  65.2 17.9 %all-gather.7.cloned.1.call-done = bf16[1,1,512,4096]{3,2,1,0:T(8,128)(2,1)} async-done(((bf16[1,1,64,4096]{3,2,1,0:T(8,128)(2,1)}), bf16[1,1,512,4096]{3,2,1,0:T(8,128)(2,1)}) %all-gather.7.cloned.1.call-update) | async-done | bytes 4194320 | tf_op jit(solution)/shard_map/all_gather | solution.py:57
  83.0 6.0 fusion.36
  89.0 2.3 fusion.56
  91.3 1.9 fusion.53
  93.2 1.8 fusion.7
  94.9 0.0 copy-done.11
  94.9 0.0 copy-start.9
  95.0 1.6 bitcast_multiply_fusion.1
  96.5 1.5 bitcast_multiply_fusion
  98.0 1.6 copy.48
  99.6 0.1 fusion.77
  99.7 1.1 pad_maximum_fusion
  100.8 1.6 copy.49
  102.4 0.0 copy-start.15
  102.4 0.0 copy-start.5
  102.4 0.0 copy-start.16
  102.4 1.3 fusion.78
  103.7 1.3 add_convert_fusion.1
  105.0 0.2 fusion.68
  105.3 0.0 copy-start.17
  105.3 0.0 slice-start
  105.3 2.3 multiply_bitcast_fusion.1
  107.7 0.0 slice-start.1
  107.7 0.0 copy-start.4
  107.7 3.5 multiply_bitcast_fusion
  111.3 16.0 %fusion.1 = f32[4096,1280]{0,1:T(8,128)} fusion(f32[4096,512]{0,1:T(8,128)S(1)} %multiply_bitcast_fusion.1, f32[4096,768]{0,1:T(8,128)S(1)} %multiply_bitcast_fusion, bf16[4096,512]{0,1:T(8,128)(2,1)S(1)} %bitcast.188, bf16[4096,768]{0,1:T(8,128)(2,1)S(1)} %bitcast.184), kind=kLoop, calls=%fused_computation.2 | loop fusion | flops 47185920 | bytes 52428800 | tf_op jit(solution)/shard_map/div | solution.py:133
  127.2 0.0 reduce-scatter.5.cloned.1.call-update
  127.3 0.0 reduce-scatter.3.cloned.1.call-start
  127.3 7.9 %multiply_convert_fusion = bf16[512,4096]{1,0:T(8,128)(2,1)} fusion(bf16[1,4096,768]{2,1,0:T(8,128)(2,1)} %param.6, bf16[512,128]{1,0:T(8,128)(2,1)S(1)} %copy-done.17, bf16[512,128]{1,0:T(8,128)(2,1)S(1)} %fusion.68, bf16[512,512]{1,0:T(8,128)(2,1)S(1)} %copy-done.14), kind=kOutput, calls=%fused_computation.5 | convolution fusion | flops 3227779072 | bytes 11272192 | tf_op jit(solution)/shard_map/dot_general | solution.py:113
  135.2 0.0 reduce-scatter.3.cloned.1.call-update
  135.2 440.8 %reduce-scatter.5.cloned.1.call-done = f32[128,1280]{0,1:T(8,128)} async-done(((f32[4096,1280]{0,1:T(8,128)}), f32[128,1280]{0,1:T(8,128)}) %reduce-scatter.5.cloned.1.call-update) | async-done | bytes 655376 | tf_op jit(solution)/shard_map/reduce_scatter | solution.py:132
  576.1 1.1 convert.26
  577.2 0.8 copy.27
  578.0 0.7 slice_bitcast_fusion.2
  578.7 40.1 %reduce-scatter.3.cloned.1.call-done = bf16[64,4096]{1,0:T(8,128)(2,1)} async-done(((bf16[512,4096]{1,0:T(8,128)(2,1)}), bf16[64,4096]{1,0:T(8,128)(2,1)}) %reduce-scatter.3.cloned.1.call-update) | async-done | bytes 524304 | tf_op jit(solution)/shard_map/reduce_scatter | solution.py:111
  (30 shorter events, 0.1 us)
Async XLA Ops:
  7.2 39.3 %all-gather.5.cloned.1.call-start = ((), (), s32[]{:S(2)}) async-start(), calls=%async_computation.4 | async-start | bytes 4718592 | tf_op jit(solution)/shard_map/all_gather | solution.py:56
  7.9 75.1 %all-gather.7.cloned.1.call-start = ((), (), s32[]{:S(2)}) async-start(), calls=%async_computation.5 | async-start | bytes 4718592 | tf_op jit(solution)/shard_map/all_gather | solution.py:57
  8.6 567.4 %reduce-scatter.5.cloned.1.call-start = ((), (), s32[]{:S(2)}) async-start(), calls=%async_computation.3 | async-start | bytes 21626880 | tf_op jit(solution)/shard_map/reduce_scatter | solution.py:132
  19.2 34.7 %copy-start.12 = (f32[512,64]{1,0:T(8,128)}, f32[512,64]{1,0:T(8,128)S(1)}, u32[]{:S(2)}) copy-start(f32[512,64]{1,0:T(8,128)S(1)} %get-tuple-element.17) | copy-start | bytes 393220
  53.7 1.1 copy-start.2
  55.1 1.5 slice-start.2
  55.3 1.0 copy-start.10
  59.5 4.8 copy-start.7
  62.3 2.0 copy-start
  83.0 6.0 copy-start.1
  83.0 6.0 copy-start.3
  83.0 6.0 copy-start.8
  93.2 1.8 copy-start.11
  94.9 1.6 copy-start.9
  99.7 5.3 copy-start.13
  102.4 2.7 copy-start.15
  102.4 2.9 copy-start.5
  102.4 2.9 copy-start.16
  105.3 2.4 copy-start.6
  105.3 2.4 copy-start.14
  105.3 2.4 copy-start.17
  105.3 5.9 slice-start
  107.7 3.5 slice-start.1
  107.7 3.5 copy-start.4
  127.3 491.6 %reduce-scatter.3.cloned.1.call-start = ((), (), s32[]{:S(2)}) async-start(), calls=%async_computation.2 | async-start | bytes 4718592 | tf_op jit(solution)/shard_map/reduce_scatter | solution.py:111
Sparse Core Ops, SparseCore 0:
  9.9 36.5 all-gather.4
  48.3 34.6 all-gather.6
  127.4 448.6 reduce-scatter.4
  579.0 39.7 reduce-scatter.2
where the time goes:
time: 629 us; the launch traced here: 625 us
  waiting for transfers between devices  528 us (84%)
  matrix products  38.7 us (6%)
  other arithmetic  25.4 us (4%)
  local copies, waits for them, and re-layouts  19.4 us (3%)
  between operations  14.2 us (2%)
    reduce_scatter x1, waiting for transfers between devices, local(): lax.psum_scatter(stepped / replica_count, ('dp', 'replica'), scatter_dime...  441 us
    reduce_scatter x1, waiting for transfers between devices, local(): lax.psum_scatter((lax.dot_general(dprojected, weight_in, (((1,), (1,)), (...  40.1 us
    all_gather x1, waiting for transfers between devices, local(): lax.all_gather(hidden_states[0, 0], 'tensor', axis=0, tiled=True)  27.3 us
    all_gather x1, waiting for transfers between devices, local(): lax.all_gather(grad_output[0, 0], 'tensor', axis=0, tiled=True)  17.9 us
    div x1, other arithmetic, local(): stepped / replica_count  16 us
  transfers between devices with their start and end apart: 4, of which 4 were waited for; matrix products, arithmetic and copies ran while one was open for 6% of the time, Pallas kernels for 0%

commit v1 on v0

v1 whole, which is shorter than its diff:
```python
import functools

import jax
import jax.numpy as jnp
import numpy as np
from jax import lax
from jax.experimental import pallas as pl
from jax.experimental.pallas import tpu as pltpu
from jax.sharding import PartitionSpec as P

D = 4096
HQ = 32
HD = 128
SEQ = 512
REPLICAS = 16
NODE_DP = 2
LEARN_RATE = 0.5
ROPE_BASE = 500000.0
MASK_VALUE = -1e30

NX, NY, NZ = 4, 4, 8

HEADS = 4
QW = HEADS * HD
IN_W = QW + 2 * HD
TOK = 64
A_ROWS = QW // 2
B_COLS = IN_W // 2
X_COLS = D // 2
CHUNK = D // (NY * NZ)
SCALE_IN = D ** (-0.5)
SCALE_OUT = (HQ * HD) ** (-0.5)
SCALE_HD = HD ** (-0.5)
W_SHARE = 1.0 / (NODE_DP * REPLICAS)
G_IN = -LEARN_RATE * SCALE_IN / REPLICAS
G_OUT = -LEARN_RATE * SCALE_OUT / REPLICAS

BF16 = jnp.bfloat16
F32 = jnp.float32


def rope_tables():
    half = HD // 2
    frequency = np.float32(ROPE_BASE) ** (
        -(np.arange(half, dtype=np.float32) * np.float32(2.0)) / np.float32(HD)
    )
    angles = np.arange(SEQ, dtype=np.float32)[:, None] * frequency[None, :].astype(np.float32)
    cosine, sine = np.cos(angles).astype(np.float32), np.sin(angles).astype(np.float32)
    return np.concatenate([cosine, cosine], 1), np.concatenate([-sine, sine], 1)


def mm(left, right):
    return lax.dot_general(left, right, (((1,), (0,)), ((), ())), preferred_element_type=F32)


def mm_nt(left, right):
    return lax.dot_general(left, right, (((1,), (1,)), ((), ())), preferred_element_type=F32)


def mm_tn(left, right):
    return lax.dot_general(left, right, (((0,), (0,)), ((), ())), preferred_element_type=F32)


def body(
    hid, gout, w_in, w_out, cos_h, sin_h,
    ig_ref, sin_ref, sout_ref,
    H, G, HT, WI, WO, COS, SIN, Q, K, V, PR, C, CT, DC, DP, DK, DV,
    a0, ar, ao, b0, br, bo, PB, igr, x0, xr,
    lsem, ag_s, ag_r, a_s, a_r, ao_s, ao_r, b_s, b_r, bo_s, bo_r, sib_s, sib_r, x_s, x_r,
):
    t = lax.axis_index("tensor")
    x, core = t // 2, t % 2
    dp = lax.axis_index("dp")
    rep = lax.axis_index("replica")
    z, ylo = rep // 2, rep % 2
    y = dp * 2 + ylo

    def x_dev(step):
        return {"tensor": ((x + step + NX) % NX) * 2 + core}

    def y_dev(step):
        other = (y + step + NY) % NY
        return {"dp": other // 2, "replica": z * 2 + other % 2}

    def z_dev(step):
        return {"replica": ((z + step + NZ) % NZ) * 2 + ylo}

    sib = {"tensor": x * 2 + 1 - core}

    def remote(src, dst, ssem, rsem, dev):
        return pltpu.make_async_remote_copy(
            src_ref=src, dst_ref=dst, send_sem=ssem, recv_sem=rsem,
            device_id=dev, device_id_type=pl.DeviceIdType.MESH,
        )

    my_rows = pl.ds(pl.multiple_of((x * 2 + core) * TOK, TOK), TOK)
    loads = [
        pltpu.make_async_copy(hid.at[0, 0], H.at[my_rows], lsem.at[0]),
        pltpu.make_async_copy(gout.at[0, 0], G.at[my_rows], lsem.at[1]),
        pltpu.make_async_copy(cos_h, COS, lsem.at[2]),
        pltpu.make_async_copy(sin_h, SIN, lsem.at[3]),
        pltpu.make_async_copy(w_in.at[0], WI, lsem.at[4]),
        pltpu.make_async_copy(w_out.at[0], WO, lsem.at[5]),
    ]
    for load in loads:
        load.start()

    barrier = pltpu.get_barrier_semaphore()
    peers = [x_dev(1), x_dev(-1), sib, y_dev(1), y_dev(-1), z_dev(1), z_dev(-1)]
    for peer in peers:
        pl.semaphore_signal(barrier, inc=1, device_id=peer, device_id_type=pl.DeviceIdType.MESH)
    pl.semaphore_wait(barrier, len(peers))

    def gather(i, shard, full):
        def rows(step, start=0, size=TOK):
            at = (((x + step + NX) % NX) * 2 + core) * TOK + start
            return full.at[pl.ds(pl.multiple_of(at, 32), size)]

        def msg(m, src, dst, dev):
            return remote(src, dst, ag_s.at[i, m], ag_r.at[i, m], dev)

        half = TOK // 2
        own = shard.at[0, 0]
        return [
            msg(0, own, rows(0), x_dev(1)),
            msg(1, own, rows(0), x_dev(-1)),
            msg(2, own, rows(0), sib),
            msg(3, rows(-1, 0, half), rows(-1, 0, half), x_dev(1)),
            msg(4, rows(-1), rows(-1), sib),
            msg(5, rows(1, half, half), rows(1, half, half), x_dev(-1)),
            msg(6, rows(1), rows(1), sib),
            msg(7, rows(2, 0, half), rows(2, 0, half), sib),
            msg(8, rows(2, half, half), rows(2, half, half), sib),
        ]

    gh = gather(0, hid, H)
    gg = gather(1, gout, G)

    def first(msgs):
        for m in (0, 1, 2):
            msgs[m].start()

    def relay(msgs):
        msgs[0].wait_recv()
        msgs[3].start()
        msgs[1].wait_recv()
        msgs[5].start()
        msgs[4].start()
        msgs[6].start()

    def last(msgs):
        msgs[3].wait_recv()
        msgs[7].start()
        msgs[5].wait_recv()
        msgs[8].start()
        for m in (2, 4, 6, 7, 8):
            msgs[m].wait_recv()

    first(gh)
    relay(gh)
    first(gg)
    for load in loads[2:]:
        load.wait()
    loads[0].wait()
    last(gh)

    cosine, sine = COS, SIN

    def rotate(v):
        return v * cosine[...] + pltpu.roll(v, HD // 2, 1) * sine[...]

    def unrotate(g):
        return g * cosine[...] + pltpu.roll(g * sine[...], HD // 2, 1)

    for n in range(3):
        proj = mm(H[...], WI[:, n * 256 : n * 256 + 256]) * SCALE_IN
        left, right = proj[:, :HD], proj[:, HD:]
        if n < 2:
            Q[:, n * 256 : n * 256 + HD] = rotate(left).astype(BF16)
            Q[:, n * 256 + HD : n * 256 + 256] = rotate(right).astype(BF16)
        else:
            K[...] = rotate(left).astype(BF16)
            V[...] = right.astype(BF16)

    @pl.loop(0, D // 256)
    def _(n):
        at = pl.multiple_of(n * 256, 256)
        HT[pl.ds(at, 256), :] = H[:, pl.ds(at, 256)].T

    RB = 128

    @pl.loop(0, HEADS)
    def _(j):
        cols = pl.ds(pl.multiple_of(j * HD, HD), HD)
        for i in range(SEQ // RB):
            r, kx = i * RB, (i + 1) * RB
            s = mm_nt(Q[r : r + RB, cols], K[:kx, :]) * SCALE_HD
            row = lax.broadcasted_iota(jnp.int32, (RB, kx), 0) + r
            col = lax.broadcasted_iota(jnp.int32, (RB, kx), 1)
            s = jnp.where(row >= col, s, MASK_VALUE)
            e = jnp.exp(s - jnp.max(s, axis=1, keepdims=True))
            p = e / jnp.sum(e, axis=1, keepdims=True)
            PR[j, r : r + RB, :kx] = p
            c = mm(p.astype(BF16), V[:kx, :]).astype(BF16)
            C[r : r + RB, cols] = c
            CT[cols, r : r + RB] = c.T

    relay(gg)
    loads[1].wait()
    last(gg)

    def chunk_of(yt, zt):
        return (yt // 2) * (2 * NZ) + zt * 2 + yt % 2

    def a_unit(d, s, h):
        sg = 1 - 2 * d
        yt = (y - sg * (1 + s) + 2 * NY) % NY
        zt = (z - sg * (1 + h) + 2 * NZ) % NZ
        cols = pl.ds(pl.multiple_of(chunk_of(yt, zt) * CHUNK, CHUNK), CHUNK)
        rows = slice(d * A_ROWS, (d + 1) * A_ROWS)
        val = mm(CT[rows, :], G[:, cols]) * G_OUT + WO[rows, cols].astype(F32) * W_SHARE

        @pl.when(h == 0)
        def _():
            a0[d, s] = val.astype(BF16)
            remote(a0.at[d, s], ar.at[d, s, 0], a_s.at[d, s, 0], a_r.at[d, s, 0], z_dev(sg)).start()

        @pl.when(h > 0)
        def _():
            slot = ar.at[d, s, h - 1]
            remote(slot, slot, a_s.at[d, s, h - 1], a_r.at[d, s, h - 1], z_dev(sg)).wait_recv()
            total = slot[...].astype(F32) + val

            @pl.when(h < NZ - 1)
            def _():
                slot[...] = total.astype(BF16)
                remote(slot, ar.at[d, s, h], a_s.at[d, s, h], a_r.at[d, s, h], z_dev(sg)).start()

            @pl.when(h == NZ - 1)
            def _():
                @pl.when(s == 0)
                def _():
                    slot[...] = total.astype(BF16)

                @pl.when(s > 0)
                def _():
                    got = ao.at[d, s - 1]
                    remote(got, got, ao_s.at[d, s - 1], ao_r.at[d, s - 1], y_dev(sg)).wait_recv()
                    slot[...] = (total + got[...].astype(F32)).astype(BF16)

                @pl.when(s < NY - 1)
                def _():
                    remote(slot, ao.at[d, s], ao_s.at[d, s], ao_r.at[d, s], y_dev(sg)).start()

                @pl.when(s == NY - 1)
                def _():
                    sout_ref[rows, :] = slot[...]

    def b_unit(d, s, h):
        sg = 1 - 2 * d
        zt = (z - sg * (1 + s) + 2 * NZ) % NZ
        yt = (y - sg * (1 + h) + 2 * NY) % NY
        rows = pl.ds(pl.multiple_of(chunk_of(yt, zt) * CHUNK, CHUNK), CHUNK)
        cols = slice(d * B_COLS, (d + 1) * B_COLS)
        val = mm(HT[rows, :], DP[:, cols]) * G_IN + WI[rows, cols].astype(F32) * W_SHARE

        @pl.when(h == 0)
        def _():
            b0[d, s] = val.astype(BF16)
            remote(b0.at[d, s], br.at[d, s, 0], b_s.at[d, s, 0], b_r.at[d, s, 0], y_dev(sg)).start()

        @pl.when(h > 0)
        def _():
            slot = br.at[d, s, h - 1]
            remote(slot, slot, b_s.at[d, s, h - 1], b_r.at[d, s, h - 1], y_dev(sg)).wait_recv()
            total = slot[...].astype(F32) + val

            @pl.when(h < NY - 1)
            def _():
                slot[...] = total.astype(BF16)
                remote(slot, br.at[d, s, h], b_s.at[d, s, h], b_r.at[d, s, h], y_dev(sg)).start()

            @pl.when(h == NY - 1)
            def _():
                @pl.when(s == 0)
                def _():
                    slot[...] = total.astype(BF16)

                @pl.when(s > 0)
                def _():
                    got = bo.at[d, s - 1]
                    remote(got, got, bo_s.at[d, s - 1], bo_r.at[d, s - 1], z_dev(sg)).wait_recv()
                    slot[...] = (total + got[...].astype(F32)).astype(BF16)

                @pl.when(s < NZ - 1)
                def _():
                    remote(slot, bo.at[d, s], bo_s.at[d, s], bo_r.at[d, s], z_dev(sg)).start()

                @pl.when(s == NZ - 1)
                def _():
                    sin_ref[:, cols] = slot[...]

    def a_round(k):
        @pl.loop(jnp.maximum(k - (NZ - 1), 0), jnp.minimum(k, NY - 1) + 1)
        def _(s):
            a_unit(0, s, k - s)
            a_unit(1, s, k - s)

    def b_round(k):
        @pl.loop(jnp.maximum(k - (NY - 1), 0), jnp.minimum(k, NZ - 1) + 1)
        def _(s):
            b_unit(0, s, k - s)
            b_unit(1, s, k - s)

    def token_rows(xt, c):
        return pl.ds(pl.multiple_of((xt * 2 + c) * TOK, TOK), TOK)

    def sib_copy(i):
        return remote(PB.at[token_rows(i, 1 - core)], igr.at[i], sib_s.at[i], sib_r.at[i], sib)

    def x_step(h):
        for d in range(2):
            sg = 1 - 2 * d
            xt = (x - sg * (1 + h) + 2 * NX) % NX
            cols = slice(d * X_COLS, (d + 1) * X_COLS)
            term = PB[token_rows(xt, core), cols].astype(F32) + igr[xt, :, cols].astype(F32)
            if h == 0:
                x0[d] = term.astype(BF16)
                src = x0.at[d]
            else:
                src = xr.at[d, h - 1]
                remote(src, src, x_s.at[d, h - 1], x_r.at[d, h - 1], x_dev(sg)).wait_recv()
                total = (term + src[...].astype(F32)).astype(BF16)
                if h == NX - 1:
                    ig_ref[0, 0, :, cols] = total
                else:
                    src[...] = total
            if h < NX - 1:
                remote(src, xr.at[d, h], x_s.at[d, h], x_r.at[d, h], x_dev(sg)).start()

    def dcontext():
        for n in range(2):
            block = slice(n * 256, n * 256 + 256)
            DC[:, block] = (mm_nt(G[...], WO[block, :]) * SCALE_OUT).astype(BF16)
        DK[...] = jnp.zeros_like(DK)
        DV[...] = jnp.zeros_like(DV)

    def backward():
        @pl.loop(0, HEADS)
        def _(j):
            cols = pl.ds(pl.multiple_of(j * HD, HD), HD)
            for i in range(SEQ // RB):
                r, kx = i * RB, (i + 1) * RB
                dc = DC[r : r + RB, cols]
                p = PR[j, r : r + RB, :kx]
                delta = jnp.sum(
                    dc.astype(F32) * C[r : r + RB, cols].astype(F32), axis=1, keepdims=True
                )
                ds = (p * (mm_nt(dc, V[:kx, :]) - delta) * SCALE_HD).astype(BF16)
                DV[:kx, :] += mm_tn(p.astype(BF16), dc)
                DK[:kx, :] += mm_tn(ds, Q[r : r + RB, cols])
                g = mm(ds, K[:kx, :])
                cs, sn = COS[r : r + RB, :], SIN[r : r + RB, :]
                DP[r : r + RB, cols] = (g * cs + pltpu.roll(g * sn, HD // 2, 1)).astype(BF16)

        DP[:, QW : QW + HD] = unrotate(DK[...]).astype(BF16)
        DP[:, QW + HD :] = DV[...].astype(BF16)

    def input_terms():
        @pl.loop(0, D // 256)
        def _(n):
            at = pl.ds(pl.multiple_of(n * 256, 256), 256)
            PB[:, at] = (mm_nt(DP[...], WI[at, :]) * SCALE_IN).astype(BF16)

        for i in range(NX):
            sib_copy(i).start()

    LAG = 2
    ROUNDS = NY + NZ - 1

    @pl.loop(0, ROUNDS + LAG)
    def _(k):
        @pl.when(k < ROUNDS)
        def _():
            a_round(k)

        pl.when(k == 0)(dcontext)
        pl.when(k == 1)(backward)

        @pl.when(k >= LAG)
        def _():
            b_round(k - LAG)

        pl.when(k == LAG)(input_terms)

        @pl.when(k == LAG + 1)
        def _():
            for i in range(NX):
                sib_copy(i).wait_recv()
            x_step(0)

        for h in range(1, NX):
            pl.when(k == LAG + 1 + 2 * h)(functools.partial(x_step, h))

    for msgs in (gh, gg):
        for m in msgs:
            m.wait_send()
    for i in range(NX):
        sib_copy(i).wait_send()
    for d in range(2):
        for h in range(NX - 1):
            src = x0.at[d]
            remote(src, src, x_s.at[d, h], x_r.at[d, h], x_dev(1)).wait_send()

        @pl.loop(0, NY)
        def _(s):
            @pl.loop(0, NZ - 1)
            def _(h):
                src = a0.at[d, s]
                remote(src, src, a_s.at[d, s, h], a_r.at[d, s, h], z_dev(1)).wait_send()

        @pl.loop(0, NY - 1)
        def _(s):
            src = a0.at[d, s]
            remote(src, src, ao_s.at[d, s], ao_r.at[d, s], y_dev(1)).wait_send()

        @pl.loop(0, NZ)
        def _(s):
            @pl.loop(0, NY - 1)
            def _(h):
                src = b0.at[d, s]
                remote(src, src, b_s.at[d, s, h], b_r.at[d, s, h], y_dev(1)).wait_send()

        @pl.loop(0, NZ - 1)
        def _(s):
            src = b0.at[d, s]
            remote(src, src, bo_s.at[d, s], bo_r.at[d, s], z_dev(1)).wait_send()


def local(hidden_states, grad_output, w_in, w_out):
    cosine, sine = rope_tables()
    dma = pltpu.SemaphoreType.DMA
    scratch = [
        pltpu.VMEM((SEQ, D), BF16),
        pltpu.VMEM((SEQ, D), BF16),
        pltpu.VMEM((D, SEQ), BF16),
        pltpu.VMEM((D, IN_W), BF16),
        pltpu.VMEM((QW, D), BF16),
        pltpu.VMEM((SEQ, HD), F32),
        pltpu.VMEM((SEQ, HD), F32),
        pltpu.VMEM((SEQ, QW), BF16),
        pltpu.VMEM((SEQ, HD), BF16),
        pltpu.VMEM((SEQ, HD), BF16),
        pltpu.VMEM((HEADS, SEQ, SEQ), F32),
        pltpu.VMEM((SEQ, QW), BF16),
        pltpu.VMEM((QW, SEQ), BF16),
        pltpu.VMEM((SEQ, QW), BF16),
        pltpu.VMEM((SEQ, IN_W), BF16),
        pltpu.VMEM((SEQ, HD), F32),
        pltpu.VMEM((SEQ, HD), F32),
        pltpu.VMEM((2, NY, A_ROWS, CHUNK), BF16),
        pltpu.VMEM((2, NY, NZ - 1, A_ROWS, CHUNK), BF16),
        pltpu.VMEM((2, NY - 1, A_ROWS, CHUNK), BF16),
        pltpu.VMEM((2, NZ, CHUNK, B_COLS), BF16),
        pltpu.VMEM((2, NZ, NY - 1, CHUNK, B_COLS), BF16),
        pltpu.VMEM((2, NZ - 1, CHUNK, B_COLS), BF16),
        pltpu.VMEM((SEQ, D), BF16),
        pltpu.VMEM((NX, TOK, D), BF16),
        pltpu.VMEM((2, TOK, X_COLS), BF16),
        pltpu.VMEM((2, NX - 1, TOK, X_COLS), BF16),
        dma((6,)),
        dma((2, 9)), dma((2, 9)),
        dma((2, NY, NZ - 1)), dma((2, NY, NZ - 1)),
        dma((2, NY - 1)), dma((2, NY - 1)),
        dma((2, NZ, NY - 1)), dma((2, NZ, NY - 1)),
        dma((2, NZ - 1)), dma((2, NZ - 1)),
        dma((NX,)), dma((NX,)),
        dma((2, NX - 1)), dma((2, NX - 1)),
    ]
    hbm = pl.BlockSpec(memory_space=pl.ANY)
    vmem = pl.BlockSpec(memory_space=pltpu.VMEM)
    return pl.pallas_call(
        body,
        out_shape=(
            jax.ShapeDtypeStruct((1, 1, TOK, D), BF16),
            jax.ShapeDtypeStruct((CHUNK, IN_W), BF16),
            jax.ShapeDtypeStruct((QW, CHUNK), BF16),
        ),
        in_specs=[hbm] * 6,
        out_specs=(vmem, vmem, vmem),
        scratch_shapes=scratch,
        compiler_params=pltpu.CompilerParams(
            collective_id=0, has_side_effects=True, vmem_limit_bytes=60 * 1024 * 1024
        ),
        cost_estimate=pl.CostEstimate(
            flops=16_000_000_000, bytes_accessed=12_000_000, transcendentals=1_000_000
        ),
    )(hidden_states, grad_output, w_in, w_out, jnp.asarray(cosine), jnp.asarray(sine))


def solution(mesh):
    in_specs = (
        P("replica", "dp", "tensor", None),
        P("replica", "dp", "tensor", None),
        P("replica", None, "tensor"),
        P("replica", "tensor", None),
    )
    out_specs = (
        P("replica", "dp", "tensor", None),
        P(("dp", "replica"), "tensor"),
        P("tensor", ("dp", "replica")),
    )
    return jax.shard_map(local, mesh=mesh, in_specs=in_specs, out_specs=out_specs, check_vma=False)
```

time: 629 us -> 143 us (0.23)
  waiting for transfers between devices: 528 us -> 0 us
  Pallas kernels: 0 us -> 135 us
  matrix products: 38.7 us -> 0 us
  other arithmetic: 25.4 us -> 0 us
  local copies, waits for them, and re-layouts: 19.4 us -> 5.05 us
  between operations: 14.2 us -> 0.64 us
    reduce_scatter x2 -> x0, waiting for transfers between devices: 481 us -> none  [the longest x1 441 us: local(): lax.psum_scatter(stepped / replica_count, ('dp', 'replica'), scatter_dime...]
    pallas_call x0 -> x1, Pallas kernels: none -> 135 us  [local(): pl.pallas_call(body, out_shape=(jax.ShapeDtypeStruct((1, 1, TOK, D), BF16...]
    all_gather x2 -> x0, waiting for transfers between devices: 45.2 us -> none  [the longest x1 27.3 us: local(): lax.all_gather(hidden_states[0, 0], 'tensor', axis=0, tiled=True)]
    dot_general x11 -> x0, matrix products: 38.7 us -> none  [the longest x1 7.9 us: local(): lax.dot_general(dprojected, weight_in, (((1,), (1,)), ((), ())), preferre...]
    div x1 -> x0, other arithmetic: 16 us -> none  [local(): stepped / replica_count]
    unnamed x42 -> x3, local copies, waits for them, and re-layouts: 12.5 us -> 5.05 us
  transfers between devices with their start and end apart: 4 -> 0, of which waited for: 4 -> 0; matrix products, arithmetic and copies ran while one was open for 6% -> 0% of each run, Pallas kernels for 0% -> 0%
where the time goes in v1:
time: 143 us; the launch traced here: 141 us
  Pallas kernels  135 us (94%)
  local copies, waits for them, and re-layouts  5.05 us (4%)
    pallas_call x1, Pallas kernels, local(): pl.pallas_call(body, out_shape=(jax.ShapeDtypeStruct((1, 1, TOK, D), BF16...  135 us
    unnamed x3, local copies, waits for them, and re-layouts  5.05 us

profile of v1, /device:TPU:2, one launch (start us, length us, event | category | flops | bytes accessed | tf_op | source)
XLA Modules:
  0.0 141.0 jit_solution(13595359820462062186)
XLA Ops:
  0.6 135.3 %shard_map.85 = (bf16[1,1,64,4096]{3,2,1,0:T(8,128)(2,1)}, bf16[128,768]{1,0:T(8,128)(2,1)}, bf16[512,128]{1,0:T(8,128)(2,1)}) custom-call(bf16[1,1,64,4096]{3,2,1,0:T(8,128)(2,1)} %hid.1, bf16[1,1,64,4096]{3,2,1,0:T(8,128)(2,1)} %gout.1, bf16[1,4096,768]{2,1,0:T(8,128)(2,1)} %w_in.1, bf16[1,512,4096]{2,1,0:T(8,128)(2,1)} %w_out.1, ...), custom_call_target="tpu_custom_call" | custom-call | flops 16000000000 | bytes 12000000 | tf_op jit(solution)/shard_map/pallas_call | solution.py:482
  135.9 1.9 %copy.12 = bf16[1,1,64,4096]{3,2,1,0:T(8,128)(2,1)} copy(bf16[1,1,64,4096]{3,2,1,0:T(8,128)(2,1)} %get-tuple-element.6) | data formatting | bytes 1048576
  137.8 1.6 %copy.13 = bf16[128,768]{1,0:T(8,128)(2,1)} copy(bf16[128,768]{1,0:T(8,128)(2,1)} %get-tuple-element.7) | data formatting | bytes 393216
  139.4 1.6 %copy.14 = bf16[512,128]{1,0:T(8,128)(2,1)} copy(bf16[512,128]{1,0:T(8,128)(2,1)} %get-tuple-element.8) | data formatting | bytes 262144

commit v2 on v1

v2 whole, which is shorter than its diff:
```python
import functools

import jax
import jax.numpy as jnp
import numpy as np
from jax import lax
from jax.experimental import pallas as pl
from jax.experimental.pallas import tpu as pltpu
from jax.sharding import PartitionSpec as P

D = 4096
HQ = 32
HD = 128
SEQ = 512
REPLICAS = 16
NODE_DP = 2
LEARN_RATE = 0.5
ROPE_BASE = 500000.0
MASK_VALUE = -1e30

NX, NY, NZ = 4, 4, 8

HEADS = 4
QW = HEADS * HD
IN_W = QW + 2 * HD
TOK = 64
A_ROWS = QW // 4
BZ_COLS, BY_COLS = 128, 256
X_COLS = D // 2
CHUNK = D // (NY * NZ)
PAIR = 2 * CHUNK
HALF_D = D // 2
SCALE_IN = D ** (-0.5)
SCALE_OUT = (HQ * HD) ** (-0.5)
SCALE_HD = HD ** (-0.5)
W_SHARE = 1.0 / (NODE_DP * REPLICAS)
G_IN = -LEARN_RATE * SCALE_IN / REPLICAS
G_OUT = -LEARN_RATE * SCALE_OUT / REPLICAS

BF16 = jnp.bfloat16
F32 = jnp.float32


def rope_tables():
    half = HD // 2
    frequency = np.float32(ROPE_BASE) ** (
        -(np.arange(half, dtype=np.float32) * np.float32(2.0)) / np.float32(HD)
    )
    angles = np.arange(SEQ, dtype=np.float32)[:, None] * frequency[None, :].astype(np.float32)
    cosine, sine = np.cos(angles).astype(np.float32), np.sin(angles).astype(np.float32)
    return np.concatenate([cosine, cosine], 1), np.concatenate([-sine, sine], 1)


def mm(left, right):
    return lax.dot_general(left, right, (((1,), (0,)), ((), ())), preferred_element_type=F32)


def mm_nt(left, right):
    return lax.dot_general(left, right, (((1,), (1,)), ((), ())), preferred_element_type=F32)


def mm_tn(left, right):
    return lax.dot_general(left, right, (((0,), (0,)), ((), ())), preferred_element_type=F32)


def body(
    hid, gout, w_in, w_out, cos_h, sin_h,
    ig_ref, sin_ref, sout_ref,
    H, G, HT, WI, WO, TA, TB, COS, SIN, Q, K, V, PR, C, CT, DC, DA, DP, DK, DV,
    az, azo, ay, ayo, bz, bzo, by, byo, igr, x0, xr,
    lsem, ag_s, ag_r, az_s, az_r, azo_s, azo_r, ay_s, ay_r, ayo_s, ayo_r,
    bz_s, bz_r, bzo_s, bzo_r, by_s, by_r, byo_s, byo_r, sib_s, sib_r, x_s, x_r,
):
    t = lax.axis_index("tensor")
    x, core = t // 2, t % 2
    dp = lax.axis_index("dp")
    rep = lax.axis_index("replica")
    z, ylo = rep // 2, rep % 2
    y = dp * 2 + ylo

    XS, YS, ZS = {}, {}, {}
    for step in (1, -1):
        other = (y + step + NY) % NY
        XS[step] = {"tensor": ((x + step + NX) % NX) * 2 + core}
        YS[step] = {"dp": other // 2, "replica": z * 2 + other % 2}
        ZS[step] = {"replica": ((z + step + NZ) % NZ) * 2 + ylo}

    def x_dev(step):
        return XS[step]

    def y_dev(step):
        return YS[step]

    def z_dev(step):
        return ZS[step]

    sib = {"tensor": x * 2 + 1 - core}

    def remote(src, dst, ssem, rsem, dev):
        return pltpu.make_async_remote_copy(
            src_ref=src, dst_ref=dst, send_sem=ssem, recv_sem=rsem,
            device_id=dev, device_id_type=pl.DeviceIdType.MESH,
        )

    def h_rows(slot, start, size):
        return H.at[pl.ds(pl.multiple_of(slot * 2 * TOK + core * TOK + start, 32), size)]

    def g_rows(slot, start, size, cols):
        at = ((x + slot - 1 + NX) % NX) * 2 * TOK + core * TOK + start
        return G.at[pl.ds(pl.multiple_of(at, 32), size), cols]

    HALF = TOK // 2
    PLAN = (
        (None, 0, HALF, 1), (None, HALF, HALF, 1), (None, HALF, HALF, -1), (None, 0, HALF, -1), (None, 0, TOK, 0),
        (0, 0, HALF, 1), (2, HALF, HALF, -1), (0, 0, TOK, 0), (2, 0, TOK, 0), (3, 0, HALF, 0), (3, HALF, HALF, 0),
    )

    def part_z(p):
        return wrap(z + 1 + p, NZ), wrap(z - 1 - p + 4 * jnp.maximum(p - 2, 0), NZ)

    def part_cols(p):
        return [
            pl.ds(pl.multiple_of(half * HALF_D + zt * PAIR, PAIR), PAIR)
            for zt in part_z(p) for half in range(2)
        ]

    def wrap(v, n):
        below = jnp.minimum(jnp.maximum(-v, 0), 1)
        above = jnp.minimum(jnp.maximum(v - (n - 1), 0), 1)
        return v + n * below - n * above

    def upper(yt):
        return jnp.minimum(jnp.maximum(yt - 1, 0), 1)

    def copies(i, m):
        slot, start, size, step = PLAN[m]
        dev = x_dev(step) if step else sib
        here = 1 if slot is None else slot
        if i == 0:
            there = h_rows((here - step) % NX, start, size)
            src = hid.at[0, 0, pl.ds(start, size)] if slot is None else h_rows(here, start, size)
            return [remote(src, there, ag_s.at[i, m], ag_r.at[i, m], dev)]
        out = []
        for cols in part_cols(i - 1):
            there = g_rows(here, start, size, cols)
            src = gout.at[0, 0, pl.ds(start, size), cols] if slot is None else there
            out.append(remote(src, there, ag_s.at[i, m], ag_r.at[i, m], dev))
        return out

    def all_bytes(i, m):
        size = PLAN[m][2]
        ref = H.at[pl.ds(0, size)] if i == 0 else G.at[pl.ds(0, size), pl.ds(0, 4 * PAIR)]
        return remote(ref, ref, ag_s.at[i, m], ag_r.at[i, m], sib)

    def start(i, *ms):
        for m in ms:
            for copy in copies(i, m):
                copy.start()

    def got(i, *ms):
        for m in ms:
            all_bytes(i, m).wait_recv()

    def sent_all(i, *ms):
        for m in ms:
            all_bytes(i, m).wait_send()

    def direct(i):
        start(i, 0, 2, 1, 3, 4)

    def relay(i):
        for m in range(4):
            got(i, (0, 2, 1, 3)[m])
            start(i, (5, 6, 7, 8)[m])

    def share(i):
        got(i, 5)
        start(i, 9)
        got(i, 6)
        start(i, 10)

    g_own = G.at[pl.ds(pl.multiple_of((x * 2 + core) * TOK, TOK), TOK)]
    loads = [
        pltpu.make_async_copy(hid.at[0, 0], h_rows(1, 0, TOK), lsem.at[0]),
        pltpu.make_async_copy(gout.at[0, 0], g_own, lsem.at[1]),
        pltpu.make_async_copy(cos_h, COS, lsem.at[2]),
        pltpu.make_async_copy(sin_h, SIN, lsem.at[3]),
        pltpu.make_async_copy(w_in.at[0], WI, lsem.at[4]),
        pltpu.make_async_copy(w_out.at[0], WO, lsem.at[5]),
    ]
    for load in loads:
        load.start()

    barrier = pltpu.get_barrier_semaphore()
    peers = [x_dev(1), x_dev(-1), sib, y_dev(1), y_dev(-1), z_dev(1), z_dev(-1)]
    for peer in peers:
        pl.semaphore_signal(barrier, inc=1, device_id=peer, device_id_type=pl.DeviceIdType.MESH)
    pl.semaphore_wait(barrier, len(peers))

    direct(0)
    relay(0)
    direct(1)
    direct(2)
    for load in loads:
        load.wait()
    got(0, 4, 7, 8)

    def rotate(v, cosine, sine):
        return v * cosine + pltpu.roll(v, HD // 2, 1) * sine

    def unrotate(g, cosine, sine):
        return g * cosine + pltpu.roll(g * sine, HD // 2, 1)

    SHARD = 2 * TOK

    def project(slots):
        lo, hi = slots[0] * SHARD, (slots[-1] + 1) * SHARD
        at = [pl.ds(pl.multiple_of(((x + s - 1 + NX) % NX) * SHARD, SHARD), SHARD) for s in slots]
        for n in range(3):
            proj = mm(H[lo:hi, :], WI[:, n * 256 : n * 256 + 256]) * SCALE_IN
            for i, rows in enumerate(at):
                own = slice(i * SHARD, (i + 1) * SHARD)
                left, right = proj[own, :HD], proj[own, HD:]
                cosine, sine = COS[rows, :], SIN[rows, :]
                if n < 2:
                    Q[rows, n * 256 : n * 256 + HD] = rotate(left, cosine, sine).astype(BF16)
                    Q[rows, n * 256 + HD : n * 256 + 256] = rotate(right, cosine, sine).astype(BF16)
                else:
                    K[rows, :] = rotate(left, cosine, sine).astype(BF16)
                    V[rows, :] = right.astype(BF16)
        for s, rows in zip(slots, at):

            @pl.loop(0, D // 512)
            def _(n):
                c = pl.ds(pl.multiple_of(n * 512, 512), 512)
                HT[c, rows] = H[s * SHARD : (s + 1) * SHARD, c].T

    project((0, 1, 2))
    share(0)
    got(0, 9, 10)
    project((3,))
    relay(1)
    direct(3)

    RB = 128

    def forward(j):
        cols = pl.ds(pl.multiple_of(j * HD, HD), HD)
        for i in range(SEQ // RB):
            r, kx = i * RB, (i + 1) * RB
            s = mm_nt(Q[r : r + RB, cols], K[:kx, :]) * SCALE_HD
            row = lax.broadcasted_iota(jnp.int32, (RB, kx), 0) + r
            col = lax.broadcasted_iota(jnp.int32, (RB, kx), 1)
            s = jnp.where(row >= col, s, MASK_VALUE)
            e = jnp.exp(s - jnp.max(s, axis=1, keepdims=True))
            p = e * (1.0 / jnp.sum(e, axis=1, keepdims=True))
            PR[j, r : r + RB, :kx] = p
            c = mm(p.astype(BF16), V[:kx, :]).astype(BF16)
            C[r : r + RB, cols] = c
            CT[cols, r : r + RB] = c.T

    @pl.loop(0, HEADS)
    def _(j):
        forward(j)

        @pl.when(j == 1)
        def _():
            relay(2)
            direct(4)
            share(1)

    relay(3)
    share(2)

    def a_terms(p):
        for cols in part_cols(p):
            upstream = G[:, cols]
            weight = WO[:, cols]
            DA[...] += mm_nt(upstream, weight)
            grad = mm(CT[...], upstream)
            TA[:, cols] = (grad * G_OUT + weight.astype(F32) * W_SHARE).astype(BF16)

    def b_terms(p):
        for rows in part_cols(p):
            grad = mm(HT[rows, :], DP[...])
            TB[rows, :] = (grad * G_IN + WI[rows, :].astype(F32) * W_SHARE).astype(BF16)

    def hops(h, n, units):
        def first():
            for block, slots, ssems, rsems, dev, out in units:
                remote(block, slots.at[0], ssems.at[0], rsems.at[0], dev).start()

        def middle():
            for block, slots, ssems, rsems, dev, out in units:
                slot = slots.at[h - 1]
                remote(slot, slot, ssems.at[h - 1], rsems.at[h - 1], dev).wait_recv()
                slot[...] = slot[...] + block[...]
                remote(slot, slots.at[h], ssems.at[h], rsems.at[h], dev).start()

        def last():
            for block, slots, ssems, rsems, dev, out in units:
                slot = slots.at[n - 2]
                remote(slot, slot, ssems.at[n - 2], rsems.at[n - 2], dev).wait_recv()
                if out is None:
                    slot[...] = slot[...] + block[...]
                else:
                    out[...] = slot[...] + block[...]

        if isinstance(h, int):
            (first if h == 0 else last if h == n - 1 else middle)()
        else:
            pl.when(h == 0)(first)
            pl.when((h > 0) & (h < n - 1))(middle)
            pl.when(h == n - 1)(last)

    def chunk_at(yt, zt):
        at = upper(yt) * (HALF_D - PAIR) + zt * PAIR + yt * CHUNK
        return pl.ds(pl.multiple_of(at, CHUNK), CHUNK)

    def pair_at(half, zt):
        return pl.ds(pl.multiple_of(half * HALF_D + zt * PAIR, PAIR), PAIR)

    def to_y(sg, h):
        return wrap(y - sg * (1 + h), NY)

    def to_z(sg, h):
        return wrap(z - sg * (1 + h), NZ)

    def z_inside(k, piece, chunk, inner, i_s, i_r, outer, o_s, o_r, out):
        units = []
        for g in range(2):
            for d in range(2):
                sg = 1 - 2 * d
                block = piece(d, pair_at(g, to_z(sg, k)))
                units.append((block, inner.at[d, g], i_s.at[d, g], i_r.at[d, g], z_dev(sg), None))
        hops(k, NZ, units)
        j = k - (NZ - 1)

        @pl.when((j >= 0) & (j < NY))
        def _():
            units = []
            for d in range(2):
                sg = 1 - 2 * d
                yt = to_y(sg, j)
                block = chunk(inner.at[d, upper(yt), NZ - 2], yt - 2 * upper(yt))
                units.append((block, outer.at[d], o_s.at[d], o_r.at[d], y_dev(sg), out(d)))
            hops(j, NY, units)

    def y_inside(k, stages, most, piece, inner, i_s, i_r, outer, o_s, o_r, out):
        for h in reversed(range(NY)):

            @pl.when((k >= h) & (k < most + h))
            def _(h=h):
                units = []
                for s in stages(k - h):
                    for d in range(2):
                        sg = 1 - 2 * d
                        block = piece(d, chunk_at(to_y(sg, h), to_z(sg, s)))
                        units.append((block, inner.at[d, s], i_s.at[d, s], i_r.at[d, s], y_dev(sg), None))
                hops(h, NY, units)

        j = k - (NY - 1)

        @pl.when((j >= 0) & (j < NZ))
        def _():
            units = []
            for d in range(2):
                sg = 1 - 2 * d
                block = inner.at[d, j, NY - 2]
                units.append((block, outer.at[d], o_s.at[d], o_r.at[d], z_dev(sg), out(d)))
            hops(j, NZ, units)

    def lanes(ref, i):
        return ref.at[:, pl.ds(pl.multiple_of(i * CHUNK, CHUNK), CHUNK)]

    def sublanes(ref, i):
        return ref.at[pl.ds(pl.multiple_of(i * CHUNK, CHUNK), CHUNK)]

    def az_rows(d):
        return slice(d * A_ROWS, (d + 1) * A_ROWS)

    def ay_rows(d):
        return slice((2 + d) * A_ROWS, (3 + d) * A_ROWS)

    def bz_cols(d):
        return slice(d * BZ_COLS, (d + 1) * BZ_COLS)

    def by_cols(d):
        return slice(2 * BZ_COLS + d * BY_COLS, 2 * BZ_COLS + (d + 1) * BY_COLS)

    def a_round(k):
        z_inside(
            k, lambda d, at: TA.at[az_rows(d), at], lanes,
            az, az_s, az_r, azo, azo_s, azo_r, lambda d: sout_ref.at[az_rows(d)],
        )
        y_inside(
            k, lambda q: (q, 6 - q + 4 * jnp.maximum(q - 2, 0)), NZ // 2,
            lambda d, at: TA.at[ay_rows(d), at],
            ay, ay_s, ay_r, ayo, ayo_s, ayo_r, lambda d: sout_ref.at[ay_rows(d)],
        )

    def b_round(k):
        z_inside(
            k, lambda d, at: TB.at[at, bz_cols(d)], sublanes,
            bz, bz_s, bz_r, bzo, bzo_s, bzo_r, lambda d: sin_ref.at[:, bz_cols(d)],
        )
        y_inside(
            k, lambda q: (q,), NZ,
            lambda d, at: TB.at[at, by_cols(d)],
            by, by_s, by_r, byo, byo_s, byo_r, lambda d: sin_ref.at[:, by_cols(d)],
        )

    PB = H

    def token_rows(xt, c):
        return pl.ds(pl.multiple_of((xt * 2 + c) * TOK, TOK), TOK)

    def sib_copy(i):
        return remote(PB.at[token_rows(i, 1 - core)], igr.at[i], sib_s.at[i], sib_r.at[i], sib)

    def x_step(h):
        if h == 0:
            for i in range(NX):
                sib_copy(i).wait_recv()
        for d in range(2):
            sg = 1 - 2 * d
            xt = (x - sg * (1 + h) + 2 * NX) % NX
            cols = slice(d * X_COLS, (d + 1) * X_COLS)
            term = PB[token_rows(xt, core), cols].astype(F32) + igr[xt, :, cols].astype(F32)
            if h == 0:
                x0[d] = term.astype(BF16)
                src = x0.at[d]
            else:
                src = xr.at[d, h - 1]
                remote(src, src, x_s.at[d, h - 1], x_r.at[d, h - 1], x_dev(sg)).wait_recv()
                total = (term + src[...].astype(F32)).astype(BF16)
                if h == NX - 1:
                    ig_ref[0, 0, :, cols] = total
                else:
                    src[...] = total
            if h < NX - 1:
                remote(src, xr.at[d, h], x_s.at[d, h], x_r.at[d, h], x_dev(sg)).start()

    def backward(heads):
        @pl.loop(*heads)
        def _(j):
            cols = pl.ds(pl.multiple_of(j * HD, HD), HD)
            for i in range(SEQ // RB):
                r, kx = i * RB, (i + 1) * RB
                dc = DC[r : r + RB, cols]
                p = PR[j, r : r + RB, :kx]
                delta = jnp.sum(
                    dc.astype(F32) * C[r : r + RB, cols].astype(F32), axis=1, keepdims=True
                )
                ds = (p * (mm_nt(dc, V[:kx, :]) - delta) * SCALE_HD).astype(BF16)
                DV[:kx, :] += mm_tn(p.astype(BF16), dc)
                DK[:kx, :] += mm_tn(ds, Q[r : r + RB, cols])
                g = mm(ds, K[:kx, :])
                turned = unrotate(g, COS[r : r + RB, :], SIN[r : r + RB, :])
                DP[r : r + RB, cols] = turned.astype(BF16)

    def backward_first():
        DC[...] = (DA[...] * SCALE_OUT).astype(BF16)
        backward((0, 2))

    def backward_last():
        backward((2, 4))
        DP[:, QW : QW + HD] = unrotate(DK[...], COS[...], SIN[...]).astype(BF16)
        DP[:, QW + HD :] = DV[...].astype(BF16)

    def input_terms(half):
        @pl.loop(half * (D // 512), (half + 1) * (D // 512))
        def _(n):
            at = pl.ds(pl.multiple_of(n * 256, 256), 256)
            PB[:, at] = (mm_nt(DP[...], WI[at, :]) * SCALE_IN).astype(BF16)

    def input_first():
        sent_all(0, 5, 6, 7, 8, 9, 10)
        input_terms(0)

    def input_last():
        input_terms(1)
        for i in range(NX):
            sib_copy(i).start()

    DA[...] = jnp.zeros_like(DA)
    DK[...] = jnp.zeros_like(DK)
    DV[...] = jnp.zeros_like(DV)

    LAG = 5
    ROUNDS = NY + NZ - 1

    @pl.loop(0, ROUNDS + LAG)
    def _(k):
        for p in range(4):

            @pl.when(k == p)
            def _():
                got(p + 1, 4, 7, 8, 9, 10)

        @pl.when(k < 4)
        def _():
            a_terms(k)

        @pl.when(k < ROUNDS)
        def _():
            a_round(k)

        @pl.when((k >= LAG) & (k < LAG + 4))
        def _():
            b_terms(k - LAG)

        @pl.when(k >= LAG)
        def _():
            b_round(k - LAG)

        @pl.when(k == 0)
        def _():
            relay(4)
            share(3)

        pl.when(k == 1)(functools.partial(share, 4))
        pl.when(k == 3)(backward_first)
        pl.when(k == 4)(backward_last)
        pl.when(k == LAG + 1)(input_first)
        pl.when(k == LAG + 2)(input_last)
        for h in range(NX):
            pl.when(k == LAG + 3 + 2 * h)(functools.partial(x_step, h))

    sent_all(0, 0, 1, 2, 3, 4)
    for i in range(1, 5):
        sent_all(i, *range(11))
    for i in range(NX):
        sib_copy(i).wait_send()

    def sent(slots, ssems, rsems):
        @pl.loop(0, ssems.shape[0])
        def _(h):
            remote(slots.at[h], slots.at[h], ssems.at[h], rsems.at[h], sib).wait_send()

    for d in range(2):
        sent(xr.at[d], x_s.at[d], x_r.at[d])
        for outer, o_s, o_r in ((azo, azo_s, azo_r), (ayo, ayo_s, ayo_r), (bzo, bzo_s, bzo_r), (byo, byo_s, byo_r)):
            sent(outer.at[d], o_s.at[d], o_r.at[d])
        for inner, i_s, i_r in ((az, az_s, az_r), (ay, ay_s, ay_r), (bz, bz_s, bz_r), (by, by_s, by_r)):

            @pl.loop(0, i_s.shape[1])
            def _(s):
                sent(inner.at[d, s], i_s.at[d, s], i_r.at[d, s])


def finish(a_ref, b_ref, c_ref, x_ref, y_ref, w_ref):
    x_ref[...] = a_ref[...]
    y_ref[...] = b_ref[...]
    w_ref[...] = c_ref[...]


def local(hidden_states, grad_output, w_in, w_out):
    cosine, sine = rope_tables()
    dma = pltpu.SemaphoreType.DMA
    scratch = [
        pltpu.VMEM((SEQ, D), BF16),
        pltpu.VMEM((SEQ, D), BF16),
        pltpu.VMEM((D, SEQ), BF16),
        pltpu.VMEM((D, IN_W), BF16),
        pltpu.VMEM((QW, D), BF16),
        pltpu.VMEM((QW, D), BF16),
        pltpu.VMEM((D, IN_W), BF16),
        pltpu.VMEM((SEQ, HD), F32),
        pltpu.VMEM((SEQ, HD), F32),
        pltpu.VMEM((SEQ, QW), BF16),
        pltpu.VMEM((SEQ, HD), BF16),
        pltpu.VMEM((SEQ, HD), BF16),
        pltpu.VMEM((HEADS, SEQ, SEQ), F32),
        pltpu.VMEM((SEQ, QW), BF16),
        pltpu.VMEM((QW, SEQ), BF16),
        pltpu.VMEM((SEQ, QW), BF16),
        pltpu.VMEM((SEQ, QW), F32),
        pltpu.VMEM((SEQ, IN_W), BF16),
        pltpu.VMEM((SEQ, HD), F32),
        pltpu.VMEM((SEQ, HD), F32),
        pltpu.VMEM((2, 2, NZ - 1, A_ROWS, PAIR), BF16),
        pltpu.VMEM((2, NY - 1, A_ROWS, CHUNK), BF16),
        pltpu.VMEM((2, NZ, NY - 1, A_ROWS, CHUNK), BF16),
        pltpu.VMEM((2, NZ - 1, A_ROWS, CHUNK), BF16),
        pltpu.VMEM((2, 2, NZ - 1, PAIR, BZ_COLS), BF16),
        pltpu.VMEM((2, NY - 1, CHUNK, BZ_COLS), BF16),
        pltpu.VMEM((2, NZ, NY - 1, CHUNK, BY_COLS), BF16),
        pltpu.VMEM((2, NZ - 1, CHUNK, BY_COLS), BF16),
        pltpu.VMEM((NX, TOK, D), BF16),
        pltpu.VMEM((2, TOK, X_COLS), BF16),
        pltpu.VMEM((2, NX - 1, TOK, X_COLS), BF16),
        dma((6,)),
        dma((5, 11)), dma((5, 11)),
    ]
    for _ in range(2):
        scratch += [dma((2, 2, NZ - 1))] * 2 + [dma((2, NY - 1))] * 2
        scratch += [dma((2, NZ, NY - 1))] * 2 + [dma((2, NZ - 1))] * 2
    scratch += [dma((NX,))] * 2 + [dma((2, NX - 1))] * 2
    hbm = pl.BlockSpec(memory_space=pl.ANY)
    vmem = pl.BlockSpec(memory_space=pltpu.VMEM)
    shapes = (
        jax.ShapeDtypeStruct((1, 1, TOK, D), BF16),
        jax.ShapeDtypeStruct((CHUNK, IN_W), BF16),
        jax.ShapeDtypeStruct((QW, CHUNK), BF16),
    )
    outs = pl.pallas_call(
        body,
        out_shape=shapes,
        in_specs=[hbm] * 6,
        out_specs=(vmem, vmem, vmem),
        scratch_shapes=scratch,
        compiler_params=pltpu.CompilerParams(
            collective_id=0, has_side_effects=True, vmem_limit_bytes=60 * 1024 * 1024
        ),
        cost_estimate=pl.CostEstimate(
            flops=16_000_000_000, bytes_accessed=12_000_000, transcendentals=1_000_000
        ),
    )(hidden_states, grad_output, w_in, w_out, jnp.asarray(cosine), jnp.asarray(sine))
    return pl.pallas_call(
        finish,
        out_shape=shapes,
        in_specs=[vmem] * 3,
        out_specs=(vmem, vmem, vmem),
    )(*outs)


def solution(mesh):
    in_specs = (
        P("replica", "dp", "tensor", None),
        P("replica", "dp", "tensor", None),
        P("replica", None, "tensor"),
        P("replica", "tensor", None),
    )
    out_specs = (
        P("replica", "dp", "tensor", None),
        P(("dp", "replica"), "tensor"),
        P("tensor", ("dp", "replica")),
    )
    return jax.shard_map(local, mesh=mesh, in_specs=in_specs, out_specs=out_specs, check_vma=False)
```

time: 143 us -> 133 us (0.930); the launches traced: 141 us -> 133 us
  local copies, waits for them, and re-layouts: 5.05 us -> 0 us
  Pallas kernels: 135 us -> 133 us
    unnamed x3 -> x0, local copies, waits for them, and re-layouts: 5.05 us -> none
    pallas_call x1 -> x2, Pallas kernels: 135 us -> 133 us  [the longest x1 130 us: local(): pl.pallas_call(body, out_shape=shapes, in_specs=[hbm] * 6, out_specs=(vme...]
where the time goes in v2:
time: 133 us
  Pallas kernels  133 us (100%)
    pallas_call x1, Pallas kernels, local(): pl.pallas_call(body, out_shape=shapes, in_specs=[hbm] * 6, out_specs=(vme...  130 us

profile of v2, /device:TPU:2, one launch (start us, length us, event | category | flops | bytes accessed | tf_op | source)
XLA Modules:
  0.0 133.2 jit_solution(7224684497734750394)
XLA Ops:
  0.6 130.5 %shard_map.85 = (bf16[1,1,64,4096]{3,2,1,0:T(8,128)(2,1)}, bf16[128,768]{1,0:T(8,128)(2,1)}, bf16[512,128]{1,0:T(8,128)(2,1)}) custom-call(bf16[1,1,64,4096]{3,2,1,0:T(8,128)(2,1)} %hid.1, bf16[1,1,64,4096]{3,2,1,0:T(8,128)(2,1)} %gout.1, bf16[1,4096,768]{2,1,0:T(8,128)(2,1)} %w_in.1, bf16[1,512,4096]{2,1,0:T(8,128)(2,1)} %w_out.1, ...), custom_call_target="tpu_custom_call" | custom-call | flops 16000000000 | bytes 12000000 | tf_op jit(solution)/shard_map/pallas_call | solution.py:607
  131.1 2.1 %shard_map.86 = (bf16[1,1,64,4096]{3,2,1,0:T(8,128)(2,1)}, bf16[128,768]{1,0:T(8,128)(2,1)}, bf16[512,128]{1,0:T(8,128)(2,1)}) custom-call(bf16[1,1,64,4096]{3,2,1,0:T(8,128)(2,1)} %get-tuple-element.6.a_ref, bf16[128,768]{1,0:T(8,128)(2,1)} %get-tuple-element.7.b_ref, bf16[512,128]{1,0:T(8,128)(2,1)} %get-tuple-element.8.c_ref), custom_call_target="tpu_custom_call" | custom-call | tf_op jit(solution)/shard_map/pallas_call | solution.py:620

commit v3 on v2

--- a/solution.py
+++ b/solution.py
@@ -116,7 +116,7 @@
     )
 
     def part_z(p):
-        return wrap(z + 1 + p, NZ), wrap(z - 1 - p + 4 * jnp.maximum(p - 2, 0), NZ)
+        return wrap(z - NZ // 2 + p, NZ), wrap(z + NZ // 2 - 1 - p, NZ)
 
     def part_cols(p):
         return [
@@ -285,33 +285,32 @@
             grad = mm(HT[rows, :], DP[...])
             TB[rows, :] = (grad * G_IN + WI[rows, :].astype(F32) * W_SHARE).astype(BF16)
 
-    def hops(h, n, units):
-        def first():
-            for block, slots, ssems, rsems, dev, out in units:
-                remote(block, slots.at[0], ssems.at[0], rsems.at[0], dev).start()
-
-        def middle():
-            for block, slots, ssems, rsems, dev, out in units:
-                slot = slots.at[h - 1]
-                remote(slot, slot, ssems.at[h - 1], rsems.at[h - 1], dev).wait_recv()
-                slot[...] = slot[...] + block[...]
-                remote(slot, slots.at[h], ssems.at[h], rsems.at[h], dev).start()
-
-        def last():
-            for block, slots, ssems, rsems, dev, out in units:
-                slot = slots.at[n - 2]
-                remote(slot, slot, ssems.at[n - 2], rsems.at[n - 2], dev).wait_recv()
-                if out is None:
-                    slot[...] = slot[...] + block[...]
-                else:
-                    out[...] = slot[...] + block[...]
-
-        if isinstance(h, int):
-            (first if h == 0 else last if h == n - 1 else middle)()
-        else:
-            pl.when(h == 0)(first)
-            pl.when((h > 0) & (h < n - 1))(middle)
-            pl.when(h == n - 1)(last)
+    def length(n, e, sg):
+        return n // 2 - (0 if (e == 0) == (sg == 1) else 1)
+
+    def step(dist, n, e, sg, block, slots, ssems, rsems, dev):
+        if dist > length(n, e, sg):
+            return
+        h = length(n, e, sg) - dist
+        i = h + (0 if sg == 1 else length(n, e, 1))
+        src = block
+        if h > 0:
+            src = slots.at[i - 1]
+            remote(src, src, ssems.at[i - 1], rsems.at[i - 1], dev).wait_recv()
+            src[...] = src[...] + block[...]
+        remote(src, slots.at[i], ssems.at[i], rsems.at[i], dev).start()
+
+    def total_at(n, e):
+        return length(n, e, 1) - 1
+
+    def last(n, e, block, slots, ssems, rsems, out=None):
+        terms = [block[...].astype(F32)]
+        for i in (total_at(n, e), n - 2):
+            slot = slots.at[i]
+            remote(slot, slot, ssems.at[i], rsems.at[i], sib).wait_recv()
+            terms.append(slot[...].astype(F32))
+        out = slots.at[total_at(n, e)] if out is None else out
+        out[...] = (terms[0] + terms[1] + terms[2]).astype(BF16)
 
     def chunk_at(yt, zt):
         at = upper(yt) * (HALF_D - PAIR) + zt * PAIR + yt * CHUNK
@@ -320,55 +319,93 @@
     def pair_at(half, zt):
         return pl.ds(pl.multiple_of(half * HALF_D + zt * PAIR, PAIR), PAIR)
 
-    def to_y(sg, h):
-        return wrap(y - sg * (1 + h), NY)
-
-    def to_z(sg, h):
-        return wrap(z - sg * (1 + h), NZ)
+    WAYS = [(e, sg) for e in range(2) for sg in (1, -1)]
 
     def z_inside(k, piece, chunk, inner, i_s, i_r, outer, o_s, o_r, out):
-        units = []
-        for g in range(2):
-            for d in range(2):
-                sg = 1 - 2 * d
-                block = piece(d, pair_at(g, to_z(sg, k)))
-                units.append((block, inner.at[d, g], i_s.at[d, g], i_r.at[d, g], z_dev(sg), None))
-        hops(k, NZ, units)
-        j = k - (NZ - 1)
-
-        @pl.when((j >= 0) & (j < NY))
-        def _():
-            units = []
-            for d in range(2):
-                sg = 1 - 2 * d
-                yt = to_y(sg, j)
-                block = chunk(inner.at[d, upper(yt), NZ - 2], yt - 2 * upper(yt))
-                units.append((block, outer.at[d], o_s.at[d], o_r.at[d], y_dev(sg), out(d)))
-            hops(j, NY, units)
-
-    def y_inside(k, stages, most, piece, inner, i_s, i_r, outer, o_s, o_r, out):
-        for h in reversed(range(NY)):
-
-            @pl.when((k >= h) & (k < most + h))
-            def _(h=h):
-                units = []
-                for s in stages(k - h):
-                    for d in range(2):
-                        sg = 1 - 2 * d
-                        block = piece(d, chunk_at(to_y(sg, h), to_z(sg, s)))
-                        units.append((block, inner.at[d, s], i_s.at[d, s], i_r.at[d, s], y_dev(sg), None))
-                hops(h, NY, units)
-
-        j = k - (NY - 1)
-
-        @pl.when((j >= 0) & (j < NZ))
-        def _():
-            units = []
-            for d in range(2):
-                sg = 1 - 2 * d
-                block = inner.at[d, j, NY - 2]
-                units.append((block, outer.at[d], o_s.at[d], o_r.at[d], z_dev(sg), out(d)))
-            hops(j, NZ, units)
+        half = NZ // 2
+
+        def inside(g):
+            for i in range(half):
+
+                @pl.when(k == i)
+                def _(dist=half - i):
+                    for e, sg in WAYS:
+                        block = piece(e, pair_at(g, wrap(z + sg * dist, NZ)))
+                        step(dist, NZ, e, sg, block, inner.at[e, g], i_s.at[e, g], i_r.at[e, g], z_dev(sg))
+
+            @pl.when(k == half)
+            def _():
+                for e in range(2):
+                    last(NZ, e, piece(e, pair_at(g, z)), inner.at[e, g], i_s.at[e, g], i_r.at[e, g])
+
+        def chunk_of(e, yt):
+            return chunk(inner.at[e, upper(yt), total_at(NZ, e)], yt - 2 * upper(yt))
+
+        def outside():
+            for dist in (2, 1):
+
+                @pl.when(k == half + 2 - dist)
+                def _(dist=dist):
+                    for e, sg in WAYS:
+                        block = chunk_of(e, wrap(y + sg * dist, NY))
+                        step(dist, NY, e, sg, block, outer.at[e], o_s.at[e], o_r.at[e], y_dev(sg))
+
+            @pl.when(k == half + 2)
+            def _():
+                for e in range(2):
+                    last(NY, e, chunk_of(e, y), outer.at[e], o_s.at[e], o_r.at[e], out(e))
+
+        return inside, outside
+
+    def y_inside(k, piece, inner, i_s, i_r, outer, o_s, o_r, out):
+        half = NZ // 2
+
+        def one(dist, s, zt):
+            for e, sg in WAYS:
+                if dist > 0:
+                    block = piece(e, chunk_at(wrap(y + sg * dist, NY), zt))
+                    step(dist, NY, e, sg, block, inner.at[e, s], i_s.at[e, s], i_r.at[e, s], y_dev(sg))
+                elif sg == 1:
+                    last(NY, e, piece(e, chunk_at(y, zt)), inner.at[e, s], i_s.at[e, s], i_r.at[e, s])
+
+        def inside(dist):
+            g = k - (2 - dist)
+
+            @pl.when((g >= 0) & (g <= half))
+            def _():
+                one(dist, half - g, wrap(z + half - g, NZ))
+
+            @pl.when((g > 0) & (g < half))
+            def _():
+                one(dist, half + g, wrap(z - half + g, NZ))
+
+        def outside():
+            for dist in range(half, 0, -1):
+
+                @pl.when(k == half + 2 - dist)
+                def _(dist=dist):
+                    for e, sg in WAYS:
+                        block = inner.at[e, dist if sg == 1 else NZ - dist, total_at(NY, e)]
+                        step(dist, NZ, e, sg, block, outer.at[e], o_s.at[e], o_r.at[e], z_dev(sg))
+
+            @pl.when(k == half + 2)
+            def _():
+                for e in range(2):
+                    block = inner.at[e, 0, total_at(NY, e)]
+                    last(NZ, e, block, outer.at[e], o_s.at[e], o_r.at[e], out(e))
+
+        return inside, outside
+
+    def both(z_part, y_part):
+        z_in, z_out = z_part
+        y_in, y_out = y_part
+        y_in(2)
+        z_in(0)
+        y_in(1)
+        z_in(1)
+        y_in(0)
+        y_out()
+        z_out()
 
     def lanes(ref, i):
         return ref.at[:, pl.ds(pl.multiple_of(i * CHUNK, CHUNK), CHUNK)]
@@ -389,26 +426,26 @@
         return slice(2 * BZ_COLS + d * BY_COLS, 2 * BZ_COLS + (d + 1) * BY_COLS)
 
     def a_round(k):
-        z_inside(
+        z_part = z_inside(
             k, lambda d, at: TA.at[az_rows(d), at], lanes,
             az, az_s, az_r, azo, azo_s, azo_r, lambda d: sout_ref.at[az_rows(d)],
         )
-        y_inside(
-            k, lambda q: (q, 6 - q + 4 * jnp.maximum(q - 2, 0)), NZ // 2,
-            lambda d, at: TA.at[ay_rows(d), at],
+        y_part = y_inside(
+            k, lambda d, at: TA.at[ay_rows(d), at],
             ay, ay_s, ay_r, ayo, ayo_s, ayo_r, lambda d: sout_ref.at[ay_rows(d)],
         )
+        both(z_part, y_part)
 
     def b_round(k):
-        z_inside(
+        z_part = z_inside(
             k, lambda d, at: TB.at[at, bz_cols(d)], sublanes,
             bz, bz_s, bz_r, bzo, bzo_s, bzo_r, lambda d: sin_ref.at[:, bz_cols(d)],
         )
-        y_inside(
-            k, lambda q: (q,), NZ,
-            lambda d, at: TB.at[at, by_cols(d)],
+        y_part = y_inside(
+            k, lambda d, at: TB.at[at, by_cols(d)],
             by, by_s, by_r, byo, byo_s, byo_r, lambda d: sin_ref.at[:, by_cols(d)],
         )
+        both(z_part, y_part)
 
     PB = H
 
@@ -488,44 +525,45 @@
     DV[...] = jnp.zeros_like(DV)
 
     LAG = 5
-    ROUNDS = NY + NZ - 1
+    ROUNDS = NY // 2 + NZ // 2 + 1
+
+    got(1, 4, 7, 8, 9, 10)
+    a_terms(0)
 
     @pl.loop(0, ROUNDS + LAG)
     def _(k):
-        for p in range(4):
-
-            @pl.when(k == p)
-            def _():
-                got(p + 1, 4, 7, 8, 9, 10)
-
-        @pl.when(k < 4)
-        def _():
-            a_terms(k)
-
         @pl.when(k < ROUNDS)
         def _():
             a_round(k)
 
-        @pl.when((k >= LAG) & (k < LAG + 4))
-        def _():
-            b_terms(k - LAG)
-
         @pl.when(k >= LAG)
         def _():
             b_round(k - LAG)
 
-        @pl.when(k == 0)
+        pl.when(k == 0)(functools.partial(share, 3))
+        for p in range(1, 4):
+
+            @pl.when(k == p - 1)
+            def _(p=p):
+                got(p + 1, 4, 7, 8, 9, 10)
+
+        @pl.when(k < 3)
         def _():
-            relay(4)
-            share(3)
-
+            a_terms(k + 1)
+
+        pl.when(k == 0)(functools.partial(relay, 4))
         pl.when(k == 1)(functools.partial(share, 4))
         pl.when(k == 3)(backward_first)
         pl.when(k == 4)(backward_last)
-        pl.when(k == LAG + 1)(input_first)
-        pl.when(k == LAG + 2)(input_last)
-        for h in range(NX):
-            pl.when(k == LAG + 3 + 2 * h)(functools.partial(x_step, h))
+
+        @pl.when((k >= LAG - 1) & (k < LAG + 3))
+        def _():
+            b_terms(k - LAG + 1)
+
+        pl.when(k == LAG)(input_first)
+        pl.when(k == LAG + 1)(input_last)
+        for h, at in enumerate((2, 3, 4, 6)):
+            pl.when(k == LAG + at)(functools.partial(x_step, h))
 
     sent_all(0, 0, 1, 2, 3, 4)
     for i in range(1, 5):

time: 133 us -> 125 us (0.940)
  Pallas kernels: 133 us -> 124 us
    pallas_call x1, Pallas kernels: 130 us -> 122 us  [local(): pl.pallas_call(body, out_shape=shapes, in_specs=[hbm] * 6, out_specs=(vme...]
where the time goes in v3:
time: 125 us; the launch traced here: 124 us
  Pallas kernels  124 us (99%)
    pallas_call x1, Pallas kernels, local(): pl.pallas_call(body, out_shape=shapes, in_specs=[hbm] * 6, out_specs=(vme...  122 us

profile of v3, /device:TPU:2, one launch (start us, length us, event | category | flops | bytes accessed | tf_op | source)
XLA Modules:
  0.0 124.4 jit_solution(976686862043208669)
XLA Ops:
  0.6 121.7 %shard_map.85 = (bf16[1,1,64,4096]{3,2,1,0:T(8,128)(2,1)}, bf16[128,768]{1,0:T(8,128)(2,1)}, bf16[512,128]{1,0:T(8,128)(2,1)}) custom-call(bf16[1,1,64,4096]{3,2,1,0:T(8,128)(2,1)} %hid.1, bf16[1,1,64,4096]{3,2,1,0:T(8,128)(2,1)} %gout.1, bf16[1,4096,768]{2,1,0:T(8,128)(2,1)} %w_in.1, bf16[1,512,4096]{2,1,0:T(8,128)(2,1)} %w_out.1, ...), custom_call_target="tpu_custom_call" | custom-call | flops 16000000000 | bytes 12000000 | tf_op jit(solution)/shard_map/pallas_call | solution.py:645
  122.3 2.1 %shard_map.86 = (bf16[1,1,64,4096]{3,2,1,0:T(8,128)(2,1)}, bf16[128,768]{1,0:T(8,128)(2,1)}, bf16[512,128]{1,0:T(8,128)(2,1)}) custom-call(bf16[1,1,64,4096]{3,2,1,0:T(8,128)(2,1)} %get-tuple-element.6.a_ref, bf16[128,768]{1,0:T(8,128)(2,1)} %get-tuple-element.7.b_ref, bf16[512,128]{1,0:T(8,128)(2,1)} %get-tuple-element.8.c_ref), custom_call_target="tpu_custom_call" | custom-call | tf_op jit(solution)/shard_map/pallas_call | solution.py:658

commit v4 on v3

--- a/solution.py
+++ b/solution.py
@@ -524,7 +524,7 @@
     DK[...] = jnp.zeros_like(DK)
     DV[...] = jnp.zeros_like(DV)
 
-    LAG = 5
+    LAG = 4
     ROUNDS = NY // 2 + NZ // 2 + 1
 
     got(1, 4, 7, 8, 9, 10)
@@ -554,7 +554,7 @@
         pl.when(k == 0)(functools.partial(relay, 4))
         pl.when(k == 1)(functools.partial(share, 4))
         pl.when(k == 3)(backward_first)
-        pl.when(k == 4)(backward_last)
+        pl.when(k == 3)(backward_last)
 
         @pl.when((k >= LAG - 1) & (k < LAG + 3))
         def _():

time: 125 us -> 124 us (level)
  no operation moved by 1% of the time
where the time goes in v4:
time: 124 us
  Pallas kernels  124 us (100%)
    pallas_call x1, Pallas kernels, local(): pl.pallas_call(body, out_shape=shapes, in_specs=[hbm] * 6, out_specs=(vme...  121 us

profile of v4, /device:TPU:2, one launch (start us, length us, event | category | flops | bytes accessed | tf_op | source)
XLA Modules:
  0.0 124.1 jit_solution(13954656690516773463)
XLA Ops:
  0.6 121.4 %shard_map.85 = (bf16[1,1,64,4096]{3,2,1,0:T(8,128)(2,1)}, bf16[128,768]{1,0:T(8,128)(2,1)}, bf16[512,128]{1,0:T(8,128)(2,1)}) custom-call(bf16[1,1,64,4096]{3,2,1,0:T(8,128)(2,1)} %hid.1, bf16[1,1,64,4096]{3,2,1,0:T(8,128)(2,1)} %gout.1, bf16[1,4096,768]{2,1,0:T(8,128)(2,1)} %w_in.1, bf16[1,512,4096]{2,1,0:T(8,128)(2,1)} %w_out.1, ...), custom_call_target="tpu_custom_call" | custom-call | flops 16000000000 | bytes 12000000 | tf_op jit(solution)/shard_map/pallas_call | solution.py:645
  122.1 2.1 %shard_map.86 = (bf16[1,1,64,4096]{3,2,1,0:T(8,128)(2,1)}, bf16[128,768]{1,0:T(8,128)(2,1)}, bf16[512,128]{1,0:T(8,128)(2,1)}) custom-call(bf16[1,1,64,4096]{3,2,1,0:T(8,128)(2,1)} %get-tuple-element.6.a_ref, bf16[128,768]{1,0:T(8,128)(2,1)} %get-tuple-element.7.b_ref, bf16[512,128]{1,0:T(8,128)(2,1)} %get-tuple-element.8.c_ref), custom_call_target="tpu_custom_call" | custom-call | tf_op jit(solution)/shard_map/pallas_call | solution.py:658
